TPU v7x, 32 devices: a whole 2x2x4 slice. The times are simulated.
32 devices in a mesh: ctx: 8 (over y, x, core), mem: 4 (over z).
Axes of the slice: x: 2, y: 2, z: 4, core: 2. Of those that a mesh axis runs over, the one named last changes fastest.
Arguments:
- queries: bfloat16 [4096, 1024], P(('ctx', 'mem')), may hold values from -6 to 6
- key_vectors: bfloat16 [4096, 1024], P(('ctx', 'mem')), may hold values from -30 to 30
- value_vectors: bfloat16 [4096, 1024], P(('ctx', 'mem')), may hold values from -30 to 30
- log_decay: bfloat16 [4096, 16], P(('ctx', 'mem')), may hold values from -1 to 0
- routes: int32 [4096, 2], P(('ctx', 'mem')), may hold values from 0 to 3, all different within a row; in each aligned block of 128 rows (0 to 127, 128 to 255, ...) at most 96 rows name the same one
- route_weight: float32 [4096, 2], P(('ctx', 'mem')), may hold values from 0.2 to 1
- out_gain: float32 [1024], replicated, may hold values from 0.5 to 1.5
Outputs:
- mixed_out: bfloat16 [4096, 1024], P(('ctx', 'mem'))
Inputs may be any that keep to these rules, and one draw needn't show every extreme that they name: `routes`: each token names 2 different memories; among the 128 tokens of one device (aligned blocks) no memory is named more than 96 times, and in every draw some memory is named exactly 96 times.
All inputs are finite; a program needn't handle non-finite values.
Results may differ from a plain program's by a relative error of at most 0.0046.
Values may be sent and summed in bfloat16 or wider, within the bound.
A program may use at most 128 MiB of HBM per device.

v0:
```python
import functools

import jax
import jax.numpy as jnp
from jax import lax
from jax.experimental import pallas as pl
from jax.experimental.pallas import tpu as pltpu
from jax.sharding import PartitionSpec as P

MESH = pl.DeviceIdType.MESH
GROUP = 8
NT = (((1,), (1,)), ((), ()))
TN = (((0,), (0,)), ((), ()))


def mm(a, b, dims=(((1,), (0,)), ((), ()))):
    return lax.dot_general(a, b, dims, preferred_element_type=jnp.float32)


def halves(x):
    high = x.astype(jnp.bfloat16)
    return high, (x - high.astype(jnp.float32)).astype(jnp.bfloat16)


def kernel(
    n_ctx, n_mem, n_heads, pad,
    q_ref, k_ref, v_ref, small_ref, gain_ref, out_ref,
    qbuf, kbuf, vbuf, tab_mine, tab, vt_buf, t_buf, fade_buf, pre_buf, inner_buf, send_buf,
    total_buf, keep_buf,
    send_sem, recv_sem, out_send, out_recv, tot_send, tot_recv,
):
    slots = n_mem + 1
    groups = n_ctx * n_mem // GROUP
    tok = q_ref.shape[0]
    half = 64
    me = lax.axis_index("ctx") * n_mem + lax.axis_index("mem")
    group = lax.div(me, GROUP)
    rank = lax.rem(me, GROUP)

    def device(block):
        return (lax.div(block, n_mem), lax.rem(block, n_mem))

    def peer(j):
        return lax.rem(rank + j, GROUP)

    def source(j):
        return lax.rem(rank + (GROUP - j), GROUP)

    def other(j):
        return lax.rem(group + j, groups)

    def origin(j):
        return lax.rem(group + (groups - j), groups)

    barrier = pltpu.get_barrier_semaphore()

    def greet(j, _):
        pl.semaphore_signal(
            barrier, inc=1, device_id=device(group * GROUP + peer(j)), device_id_type=MESH
        )
        return 0

    def greet_group(j, _):
        pl.semaphore_signal(
            barrier, inc=1, device_id=device(other(j) * GROUP + rank), device_id_type=MESH
        )
        return 0

    lax.fori_loop(1, GROUP, greet, 0)
    lax.fori_loop(1, groups, greet_group, 0)

    decay = small_ref[0:n_heads, :]
    first, second = small_ref[n_heads : n_heads + 1, :], small_ref[n_heads + 1 : n_heads + 2, :]
    w_first = small_ref[n_heads + 2 : n_heads + 3, :]
    w_second = small_ref[n_heads + 3 : n_heads + 4, :]
    row = lax.broadcasted_iota(jnp.int32, (tok, tok), 0)
    col = lax.broadcasted_iota(jnp.int32, (tok, tok), 1)
    causal = row <= col
    upper = jnp.where(causal, 1.0, 0.0).astype(jnp.bfloat16)
    tab_mine[...] = jnp.zeros_like(tab_mine)
    for m in range(slots):
        if m == 0:
            masked, weight = decay, jnp.ones_like(w_first)
        else:
            in_first, in_second = first == float(m - 1), second == float(m - 1)
            masked = jnp.where(in_first | in_second, decay, 0.0)
            weight = jnp.where(in_first, w_first, jnp.where(in_second, w_second, 0.0))
        cumul = mm(masked.astype(jnp.bfloat16), upper)
        for p in range(GROUP):
            for h in range(2):
                tab_mine[p, h * pad + m : h * pad + m + 1, :] = cumul[2 * p + h : 2 * p + h + 1, :]
            tab_mine[p, 2 * pad + m : 2 * pad + m + 1, :] = weight

    pl.semaphore_wait(barrier, GROUP - 1 + groups - 1)

    def columns(ref, r):
        return ref.at[:, pl.ds(pl.multiple_of(r * 128, 128), 128)]

    def transfer(kind, j, to, slot_of):
        src, dst = {
            0: lambda: (tab_mine.at[to], tab.at[slot_of]),
            1: lambda: (columns(k_ref, to), kbuf.at[slot_of]),
            2: lambda: (columns(v_ref, to), vbuf.at[slot_of]),
            3: lambda: (columns(q_ref, to), qbuf.at[slot_of]),
        }[kind]()
        return pltpu.make_async_remote_copy(
            src_ref=src,
            dst_ref=dst,
            send_sem=send_sem.at[kind, j],
            recv_sem=recv_sem.at[kind, j],
            device_id=device(group * GROUP + to),
            device_id_type=MESH,
        )

    for kind in range(4):

        def launch(j, _, kind=kind):
            transfer(kind, j, peer(j), rank).start()
            return 0

        lax.fori_loop(1, GROUP, launch, 0)

    tab[rank] = tab_mine[rank]
    own = pl.ds(pl.multiple_of(rank * 128, 128), 128)
    kbuf[rank] = k_ref[:, own]
    vbuf[rank] = v_ref[:, own]
    qbuf[rank] = q_ref[:, own]

    left = lax.broadcasted_iota(jnp.int32, (1, 128), 1) < half

    def factors(i):
        weight = tab[i, 2 * pad : 3 * pad, :]
        return [(tab[i, h * pad : (h + 1) * pad, :], weight) for h in range(2)]

    def gather_state(j, _):
        i = source(j)

        @pl.when(j > 0)
        def _():
            for kind in range(3):
                transfer(kind, j, peer(j), rank).wait_recv()

        keys = kbuf[i]
        vt = vbuf[i].astype(jnp.float32).T
        vt_buf[i] = vt.astype(jnp.bfloat16)
        parts, fades = [], []
        for h, (cumul, weight) in enumerate(factors(i)):
            last = cumul[:, tok - 1 : tok]
            faded = jnp.where(weight > 0.0, jnp.exp(last - cumul), 0.0)
            mine = vt[h * half : (h + 1) * half, :]
            scaled = jnp.concatenate([mine * faded[m : m + 1, :] for m in range(slots)], axis=0)
            parts.append(mm(scaled.astype(jnp.bfloat16), keys))
            fades.append(jnp.broadcast_to(jnp.exp(last), (pad, 128)))
        t_buf[i] = jnp.where(left, parts[0], parts[1])
        fade_buf[i] = jnp.where(left, fades[0], fades[1])
        return 0

    lax.fori_loop(0, GROUP, gather_state, 0)

    for m in range(slots):
        rows = pl.ds(m * half, half)
        state = jnp.zeros((half, 128), jnp.float32)
        kept = jnp.ones((1, 128), jnp.float32)
        for i in range(GROUP):
            fade = fade_buf[i, m : m + 1, :]
            added = t_buf[i, rows, :]
            t_buf[i, rows, :] = state
            pre_buf[i, m : m + 1, :] = kept
            state = fade * state + added
            kept = kept * fade
        total_buf[group, rows, :] = state.astype(jnp.bfloat16)
        keep_buf[group, m : m + 1, :] = kept

    def exchange(j):
        to = device(other(j) * GROUP + rank)
        return [
            pltpu.make_async_remote_copy(
                src_ref=ref.at[group],
                dst_ref=ref.at[group],
                send_sem=tot_send.at[kind, j],
                recv_sem=tot_recv.at[kind, j],
                device_id=to,
                device_id_type=MESH,
            )
            for kind, ref in enumerate((total_buf, keep_buf))
        ]

    def launch_totals(j, _):
        for copy in exchange(j):
            copy.start()
        return 0

    lax.fori_loop(1, groups, launch_totals, 0)

    def two_heads(i):
        queries = qbuf[i]
        zero = jnp.zeros_like(queries)
        return jnp.concatenate(
            [jnp.where(left, queries, zero), jnp.where(left, zero, queries)], axis=0
        )

    def inside(j, _):
        i = source(j)

        @pl.when(j > 0)
        def _():
            transfer(3, j, peer(j), rank).wait_recv()

        scores = mm(kbuf[i], two_heads(i), NT)
        for h, (cumul, weight) in enumerate(factors(i)):
            middle = 0.5 * cumul[:, tok - 1 : tok]
            read_hi, read_lo = halves(weight * jnp.exp(cumul - middle))
            write_hi, write_lo = halves(jnp.where(weight > 0.0, jnp.exp(middle - cumul), 0.0))
            factor = mm(
                jnp.concatenate([write_hi, write_lo, write_hi], axis=0),
                jnp.concatenate([read_hi, read_hi, read_lo], axis=0),
                TN,
            )
            part = scores[:, h * tok : (h + 1) * tok] * factor
            part = jnp.where(causal, part, 0.0).astype(jnp.bfloat16)
            inner_buf[i, :, h * tok : (h + 1) * tok] = mm(
                vt_buf[i, h * half : (h + 1) * half, :], part
            )
        return 0

    lax.fori_loop(0, GROUP, inside, 0)

    def await_totals(j, _):
        for copy in exchange(j):
            copy.wait_recv()
        return 0

    lax.fori_loop(1, groups, await_totals, 0)

    def carry(g, state):
        parts = []
        for m in range(slots):
            before = state[m * half : (m + 1) * half, :]
            new = keep_buf[g, m : m + 1, :] * before + total_buf[
                g, m * half : (m + 1) * half, :
            ].astype(jnp.float32)
            parts.append(jnp.where(g < group, new, before))
        return jnp.concatenate(parts, axis=0)

    carried = lax.fori_loop(0, groups, carry, jnp.zeros((slots * half, 128), jnp.float32))
    gain = gain_ref[rank]

    def give_back(j):
        to = peer(j)
        return pltpu.make_async_remote_copy(
            src_ref=send_buf.at[to],
            dst_ref=columns(out_ref, rank),
            send_sem=out_send.at[j],
            recv_sem=out_recv.at[j],
            device_id=device(group * GROUP + to),
            device_id_type=MESH,
        )

    def finish(step, _):
        j = GROUP - 1 - step
        i = peer(j)
        state = jnp.concatenate(
            [
                t_buf[i, m * half : (m + 1) * half, :]
                + pre_buf[i, m : m + 1, :] * carried[m * half : (m + 1) * half, :]
                for m in range(slots)
            ],
            axis=0,
        )
        read = mm(state.astype(jnp.bfloat16), two_heads(i), NT)
        level = jnp.concatenate(
            [weight * jnp.exp(cumul) for cumul, weight in factors(i)], axis=1
        )
        total = inner_buf[i]
        for m in range(slots):
            total = total + level[m : m + 1, :] * read[m * half : (m + 1) * half, :]
        scale = lax.rsqrt(jnp.mean(total * total, axis=0, keepdims=True) + 1e-06)
        normed = total * scale
        flat = jnp.concatenate([normed[:, :tok], normed[:, tok:]], axis=0)
        send_buf[i] = (flat.T * gain).astype(jnp.bfloat16)

        @pl.when(j > 0)
        def _():
            give_back(j).start()

        return 0

    lax.fori_loop(0, GROUP, finish, 0)
    out_ref[:, own] = send_buf[rank]

    def drain(j, _):
        for kind in range(4):
            transfer(kind, j, peer(j), rank).wait_send()
        copy = give_back(j)
        copy.wait_send()
        copy.wait_recv()
        return 0

    lax.fori_loop(1, GROUP, drain, 0)

    def drain_totals(j, _):
        for copy in exchange(j):
            copy.wait_send()
        return 0

    lax.fori_loop(1, groups, drain_totals, 0)


def on_device(queries, key_vectors, value_vectors, log_decay, routes, route_weight, out_gain):
    n_ctx, n_mem = lax.axis_size("ctx"), lax.axis_size("mem")
    tok, width = queries.shape
    heads = log_decay.shape[1]
    groups = n_ctx * n_mem // GROUP
    slots = n_mem + 1
    pad = (slots + 7) // 8 * 8
    small = jnp.concatenate(
        [
            log_decay.astype(jnp.float32),
            routes.astype(jnp.float32),
            route_weight,
            jnp.zeros((tok, 4), jnp.float32),
        ],
        axis=1,
    ).T
    gain = out_gain.reshape(GROUP, 1, 128)
    vmem = pl.BlockSpec(memory_space=pltpu.VMEM)
    return pl.pallas_call(
        functools.partial(kernel, n_ctx, n_mem, heads, pad),
        out_shape=jax.ShapeDtypeStruct((tok, width), jnp.bfloat16),
        in_specs=[vmem] * 5,
        out_specs=vmem,
        scratch_shapes=[
            pltpu.VMEM((GROUP, tok, 128), jnp.bfloat16),
            pltpu.VMEM((GROUP, tok, 128), jnp.bfloat16),
            pltpu.VMEM((GROUP, tok, 128), jnp.bfloat16),
            pltpu.VMEM((GROUP, 3 * pad, tok), jnp.float32),
            pltpu.VMEM((GROUP, 3 * pad, tok), jnp.float32),
            pltpu.VMEM((GROUP, 128, tok), jnp.bfloat16),
            pltpu.VMEM((GROUP, slots * 64, 128), jnp.float32),
            pltpu.VMEM((GROUP, pad, 128), jnp.float32),
            pltpu.VMEM((GROUP, pad, 128), jnp.float32),
            pltpu.VMEM((GROUP, 64, 2 * tok), jnp.float32),
            pltpu.VMEM((GROUP, tok, 128), jnp.bfloat16),
            pltpu.VMEM((groups, slots * 64, 128), jnp.bfloat16),
            pltpu.VMEM((groups, pad, 128), jnp.float32),
            pltpu.SemaphoreType.DMA((4, GROUP)),
            pltpu.SemaphoreType.DMA((4, GROUP)),
            pltpu.SemaphoreType.DMA((GROUP,)),
            pltpu.SemaphoreType.DMA((GROUP,)),
            pltpu.SemaphoreType.DMA((2, groups)),
            pltpu.SemaphoreType.DMA((2, groups)),
        ],
        compiler_params=pltpu.CompilerParams(
            collective_id=0, has_side_effects=True, vmem_limit_bytes=48 * 1024 * 1024
        ),
        cost_estimate=pl.CostEstimate(
            flops=2 * GROUP * 128 * 128 * 128 * 20, bytes_accessed=4 << 20, transcendentals=0
        ),
    )(queries, key_vectors, value_vectors, small, gain)


def solution(mesh):
    rows = P(("ctx", "mem"), None)
    return jax.shard_map(
        on_device,
        mesh=mesh,
        in_specs=(rows, rows, rows, rows, rows, rows, P()),
        out_specs=rows,
        check_vma=False,
    )
```

profile of v0, /device:TPU:0, one launch (start us, length us, event | category | flops | bytes accessed | tf_op | source)
XLA Modules:
  0.0 43.1 jit_solution(3083900227790347045)
XLA Ops:
  0.0 0.0 copy-start.4
  0.0 0.0 copy-start.6
  0.0 0.1 pad.3.clone
  0.1 0.6 %copy-done.6 = s32[128,2]{0,1:T(2,128)S(1)} copy-done((s32[128,2]{0,1:T(2,128)S(1)}, s32[128,2]{0,1:T(2,128)}, u32[]{:S(2)}) %copy-start.6) | copy-done | bytes 1048
  0.7 0.0 copy-done.4
  0.7 0.0 copy-start.5
  0.7 0.7 %copy-done.5 = f32[128,2]{0,1:T(2,128)S(1)} copy-done((f32[128,2]{0,1:T(2,128)S(1)}, f32[128,2]{0,1:T(2,128)}, u32[]{:S(2)}) %copy-start.5) | copy-done | bytes 1048
  1.4 0.0 copy-start.3
  1.4 0.1 maximum_bitcast_fusion.small_ref
  1.5 0.6 %copy-done.3 = f32[1024]{0:T(1024)S(1)} copy-done((f32[1024]{0:T(1024)S(1)}, f32[1024]{0:T(1024)}, u32[]{:S(2)}) %copy-start.3) | copy-done | bytes 4120
  2.1 0.0 copy-start
  2.1 0.9 %copy-done = bf16[128,1024]{1,0:T(8,128)(2,1)S(1)} copy-done((bf16[128,1024]{1,0:T(8,128)(2,1)S(1)}, bf16[128,1024]{1,0:T(8,128)(2,1)}, u32[]{:S(2)}) %copy-start) | copy-done | bytes 262168
  3.0 0.0 copy-start.1
  3.0 0.9 %copy-done.1 = bf16[128,1024]{1,0:T(8,128)(2,1)S(1)} copy-done((bf16[128,1024]{1,0:T(8,128)(2,1)S(1)}, bf16[128,1024]{1,0:T(8,128)(2,1)}, u32[]{:S(2)}) %copy-start.1) | copy-done | bytes 262168
  4.0 0.0 copy-start.2
  4.0 0.9 %copy-done.2 = bf16[128,1024]{1,0:T(8,128)(2,1)S(1)} copy-done((bf16[128,1024]{1,0:T(8,128)(2,1)S(1)}, bf16[128,1024]{1,0:T(8,128)(2,1)}, u32[]{:S(2)}) %copy-start.2) | copy-done | bytes 262168
  4.9 37.5 %shard_map.73 = bf16[128,1024]{1,0:T(8,128)(2,1)S(1)} custom-call(bf16[128,1024]{1,0:T(8,128)(2,1)S(1)} %copy-done, bf16[128,1024]{1,0:T(8,128)(2,1)S(1)} %copy-done.1, bf16[128,1024]{1,0:T(8,128)(2,1)S(1)} %copy-done.2, f32[24,128]{1,0:T(8,128)S(1)} %maximum_bitcast_fusion.small_ref, f32[8,1,128]{2,1,0:T(1,128)S(1)} %bitcast.3), custom_call_target="tpu_custom_call" | custom-call | flops 671088640 | bytes 4194304 | tf_op jit(solution)/shard_map/pallas_call | solution.py:327
  42.4 0.7 %copy.9 = bf16[128,1024]{1,0:T(8,128)(2,1)} copy(bf16[128,1024]{1,0:T(8,128)(2,1)S(1)} %shard_map.73) | data formatting | bytes 524288
  (3 shorter events, 0.0 us)
Async XLA Ops:
  0.0 0.7 %copy-start.4 = (bf16[128,16]{0,1:T(8,128)(2,1)S(1)}, bf16[128,16]{0,1:T(8,128)(2,1)}, u32[]{:S(2)}) copy-start(bf16[128,16]{0,1:T(8,128)(2,1)} %param.10) | copy-start | bytes 12292
  0.0 0.7 %copy-start.6 = (s32[128,2]{0,1:T(2,128)S(1)}, s32[128,2]{0,1:T(2,128)}, u32[]{:S(2)}) copy-start(s32[128,2]{0,1:T(2,128)} %param.11) | copy-start | bytes 3076
  0.7 0.7 %copy-start.5 = (f32[128,2]{0,1:T(2,128)S(1)}, f32[128,2]{0,1:T(2,128)}, u32[]{:S(2)}) copy-start(f32[128,2]{0,1:T(2,128)} %param.12) | copy-start | bytes 3076
  1.4 0.7 %copy-start.3 = (f32[1024]{0:T(1024)S(1)}, f32[1024]{0:T(1024)}, u32[]{:S(2)}) copy-start(f32[1024]{0:T(1024)} %param.13) | copy-start | bytes 12292
  2.1 0.9 %copy-start = (bf16[128,1024]{1,0:T(8,128)(2,1)S(1)}, bf16[128,1024]{1,0:T(8,128)(2,1)}, u32[]{:S(2)}) copy-start(bf16[128,1024]{1,0:T(8,128)(2,1)} %q_ref.1) | copy-start | bytes 786436
  3.0 0.9 %copy-start.1 = (bf16[128,1024]{1,0:T(8,128)(2,1)S(1)}, bf16[128,1024]{1,0:T(8,128)(2,1)}, u32[]{:S(2)}) copy-start(bf16[128,1024]{1,0:T(8,128)(2,1)} %k_ref.1) | copy-start | bytes 786436
  4.0 0.9 %copy-start.2 = (bf16[128,1024]{1,0:T(8,128)(2,1)S(1)}, bf16[128,1024]{1,0:T(8,128)(2,1)}, u32[]{:S(2)}) copy-start(bf16[128,1024]{1,0:T(8,128)(2,1)} %v_ref.1) | copy-start | bytes 786436
where the time goes:
time: 43.6 us; the launch traced here: 43.1 us
  Pallas kernels  37.5 us (86%)
  local copies, waits for them, and re-layouts  5.54 us (13%)
    pallas_call x1, Pallas kernels, on_device(): pl.pallas_call(functools.partial(kernel, n_ctx, n_mem, heads, pad), out_s...  37.5 us
    unnamed x15, local copies, waits for them, and re-layouts  5.46 us

commit v1 on v0

v1 whole, which is shorter than its diff:
```python
import functools

import jax
import jax.numpy as jnp
from jax import lax
from jax.experimental import pallas as pl
from jax.experimental.pallas import tpu as pltpu
from jax.sharding import PartitionSpec as P

MESH = pl.DeviceIdType.MESH
GROUP = 8
NT = (((1,), (1,)), ((), ()))
TN = (((0,), (0,)), ((), ()))


def mm(a, b, dims=(((1,), (0,)), ((), ()))):
    return lax.dot_general(a, b, dims, preferred_element_type=jnp.float32)


def halves(x):
    high = x.astype(jnp.bfloat16)
    return high, (x - high.astype(jnp.float32)).astype(jnp.bfloat16)


def kernel(
    n_ctx, n_mem, n_heads, pad,
    q_ref, k_ref, v_ref, decay_ref, routes_ref, weight_ref, gain_ref, out_ref,
    qbuf, kbuf, vbuf, tab_mine, tab, vt_buf, t_buf, fade_buf, pre_buf, inner_buf, send_buf,
    total_buf, keep_buf, decay_buf, routes_buf, weight_buf, gain_buf,
    send_sem, recv_sem, out_send, out_recv, tot_send, tot_recv, own_sem, small_sem,
):
    slots = n_mem + 1
    groups = n_ctx * n_mem // GROUP
    tok = q_ref.shape[0]
    half = 64
    me = lax.axis_index("ctx") * n_mem + lax.axis_index("mem")
    group = lax.div(me, GROUP)
    rank = lax.rem(me, GROUP)

    def device(block):
        return (lax.div(block, n_mem), lax.rem(block, n_mem))

    def flipped(j):
        partner = rank
        for bit in (1, 2, 4):
            if j & bit:
                partner = partner + bit - 2 * bit * lax.rem(lax.div(rank, bit), 2)
        return partner

    peers = [flipped(j) for j in range(GROUP)]
    devices = [device(group * GROUP + r) for r in peers]

    def other(j):
        return lax.rem(group + j, groups)

    small = [
        pltpu.make_async_copy(src, dst, small_sem.at[i])
        for i, (src, dst) in enumerate(
            (
                (decay_ref, decay_buf),
                (routes_ref, routes_buf),
                (weight_ref, weight_buf),
                (gain_ref, gain_buf),
            )
        )
    ]
    for copy in small:
        copy.start()

    def columns(ref, r):
        return ref.at[:, pl.ds(pl.multiple_of(r * 128, 128), 128)]

    own = [
        pltpu.make_async_copy(columns(src, rank), dst.at[rank], own_sem.at[i])
        for i, (src, dst) in enumerate(((k_ref, kbuf), (v_ref, vbuf), (q_ref, qbuf)))
    ]
    for copy in own:
        copy.start()

    barrier = pltpu.get_barrier_semaphore()
    for j in range(1, GROUP):
        pl.semaphore_signal(barrier, inc=1, device_id=devices[j], device_id_type=MESH)

    def greet_group(j, _):
        pl.semaphore_signal(
            barrier, inc=1, device_id=device(other(j) * GROUP + rank), device_id_type=MESH
        )
        return 0

    lax.fori_loop(1, groups, greet_group, 0)

    row = lax.broadcasted_iota(jnp.int32, (tok, tok), 0)
    col = lax.broadcasted_iota(jnp.int32, (tok, tok), 1)
    causal = row <= col
    upper = jnp.where(causal, 1.0, 0.0).astype(jnp.bfloat16)
    tab_mine[...] = jnp.zeros_like(tab_mine)
    for copy in small:
        copy.wait()
    decay = decay_buf[...].astype(jnp.float32)
    first, second = routes_buf[0:1, :], routes_buf[1:2, :]
    w_first, w_second = weight_buf[0:1, :], weight_buf[1:2, :]
    for m in range(slots):
        if m == 0:
            masked, weight = decay, jnp.ones_like(w_first)
        else:
            in_first, in_second = first == m - 1, second == m - 1
            masked = jnp.where(in_first | in_second, decay, 0.0)
            weight = jnp.where(in_first, w_first, jnp.where(in_second, w_second, 0.0))
        cumul = mm(masked.astype(jnp.bfloat16), upper)
        for p in range(GROUP):
            for h in range(2):
                tab_mine[p, h * pad + m : h * pad + m + 1, :] = cumul[2 * p + h : 2 * p + h + 1, :]
            tab_mine[p, 2 * pad + m : 2 * pad + m + 1, :] = weight

    pl.semaphore_wait(barrier, GROUP - 1 + groups - 1)

    def transfer(kind, j):
        to = peers[j]
        src, dst = {
            0: lambda: (tab_mine.at[to], tab.at[rank]),
            1: lambda: (columns(k_ref, to), kbuf.at[rank]),
            2: lambda: (columns(v_ref, to), vbuf.at[rank]),
            3: lambda: (columns(q_ref, to), qbuf.at[rank]),
        }[kind]()
        return pltpu.make_async_remote_copy(
            src_ref=src,
            dst_ref=dst,
            send_sem=send_sem.at[kind, j],
            recv_sem=recv_sem.at[kind, j],
            device_id=devices[j],
            device_id_type=MESH,
        )

    far_first = (2, 6, 3, 7, 1, 5, 4)
    for kinds in ((0, 1, 2), (3,)):
        for j in far_first:
            for kind in kinds:
                transfer(kind, j).start()

    tab[rank] = tab_mine[rank]

    left = lax.broadcasted_iota(jnp.int32, (1, 128), 1) < half

    def split(x, axis):
        zero = jnp.zeros_like(x)
        return jnp.concatenate([jnp.where(left, x, zero), jnp.where(left, zero, x)], axis=axis)

    def factors(i):
        weight = tab[i, 2 * pad : 3 * pad, :]
        return [(tab[i, h * pad : (h + 1) * pad, :], weight) for h in range(2)]

    steps = ((0, 4), (1, 5), (2, 6), (3, 7))

    def gather_state(i):
        vt = vbuf[i].astype(jnp.float32).T
        vt_buf[i] = vt.astype(jnp.bfloat16)
        parts, fades = [], []
        for h, (cumul, weight) in enumerate(factors(i)):
            last = cumul[:, tok - 1 : tok]
            faded = jnp.where(weight > 0.0, jnp.exp(last - cumul), 0.0)
            mine = vt[h * half : (h + 1) * half, :]
            parts.append(
                jnp.concatenate([mine * faded[m : m + 1, :] for m in range(slots)], axis=0)
            )
            fades.append(jnp.broadcast_to(jnp.exp(last), (pad, 128)))
        scaled = jnp.concatenate(parts, axis=1).astype(jnp.bfloat16)
        t_buf[i] = mm(scaled, split(kbuf[i], 0))
        fade_buf[i] = jnp.where(left, fades[0], fades[1])

    for step in steps:
        for j in step:
            if j == 0:
                own[0].wait()
                own[1].wait()
            else:
                for kind in range(3):
                    transfer(kind, j).wait_recv()
        for j in step:
            gather_state(peers[j])

    for m in range(slots):
        rows = pl.ds(m * half, half)
        state = jnp.zeros((half, 128), jnp.float32)
        kept = jnp.ones((1, 128), jnp.float32)
        for i in range(GROUP):
            fade = fade_buf[i, m : m + 1, :]
            added = t_buf[i, rows, :]
            t_buf[i, rows, :] = state
            pre_buf[i, m : m + 1, :] = kept
            state = fade * state + added
            kept = kept * fade
        total_buf[group, rows, :] = state.astype(jnp.bfloat16)
        keep_buf[group, m : m + 1, :] = kept

    def exchange(j):
        to = device(other(j) * GROUP + rank)
        return [
            pltpu.make_async_remote_copy(
                src_ref=ref.at[group],
                dst_ref=ref.at[group],
                send_sem=tot_send.at[kind, j],
                recv_sem=tot_recv.at[kind, j],
                device_id=to,
                device_id_type=MESH,
            )
            for kind, ref in enumerate((total_buf, keep_buf))
        ]

    def launch_totals(j, _):
        for copy in exchange(j):
            copy.start()
        return 0

    lax.fori_loop(1, groups, launch_totals, 0)

    def inside(i):
        scores = mm(kbuf[i], split(qbuf[i], 0), NT)
        for h, (cumul, weight) in enumerate(factors(i)):
            middle = 0.5 * cumul[:, tok - 1 : tok]
            read_hi, read_lo = halves(weight * jnp.exp(cumul - middle))
            write_hi, write_lo = halves(jnp.where(weight > 0.0, jnp.exp(middle - cumul), 0.0))
            factor = mm(
                jnp.concatenate([write_hi, write_lo, write_hi], axis=0),
                jnp.concatenate([read_hi, read_hi, read_lo], axis=0),
                TN,
            )
            part = scores[:, h * tok : (h + 1) * tok] * factor
            part = jnp.where(causal, part, 0.0).astype(jnp.bfloat16)
            inner_buf[i, :, h * tok : (h + 1) * tok] = mm(
                vt_buf[i, h * half : (h + 1) * half, :], part
            )

    for step in steps:
        for j in step:
            if j == 0:
                own[2].wait()
            else:
                transfer(3, j).wait_recv()
        for j in step:
            inside(peers[j])

    def await_totals(j, _):
        for copy in exchange(j):
            copy.wait_recv()
        return 0

    lax.fori_loop(1, groups, await_totals, 0)

    def carry(g, state):
        parts = []
        for m in range(slots):
            before = state[m * half : (m + 1) * half, :]
            new = keep_buf[g, m : m + 1, :] * before + total_buf[
                g, m * half : (m + 1) * half, :
            ].astype(jnp.float32)
            parts.append(jnp.where(g < group, new, before))
        return jnp.concatenate(parts, axis=0)

    carry_buf = jnp.zeros((slots * half, 128), jnp.float32)
    carried = lax.fori_loop(0, groups, carry, carry_buf)
    gain = gain_buf[rank]

    def give_back(j):
        return pltpu.make_async_remote_copy(
            src_ref=send_buf.at[peers[j]],
            dst_ref=columns(out_ref, rank),
            send_sem=out_send.at[j],
            recv_sem=out_recv.at[j],
            device_id=devices[j],
            device_id_type=MESH,
        )

    def finish(i):
        state = jnp.concatenate(
            [
                t_buf[i, m * half : (m + 1) * half, :]
                + pre_buf[i, m : m + 1, :] * carried[m * half : (m + 1) * half, :]
                for m in range(slots)
            ],
            axis=0,
        )
        read = mm(state.astype(jnp.bfloat16), split(qbuf[i], 0), NT)
        level = jnp.concatenate(
            [weight * jnp.exp(cumul) for cumul, weight in factors(i)], axis=1
        )
        total = inner_buf[i]
        for m in range(slots):
            total = total + level[m : m + 1, :] * read[m * half : (m + 1) * half, :]
        scale = lax.rsqrt(jnp.mean(total * total, axis=0, keepdims=True) + 1e-06)
        normed = total * scale
        flat = jnp.concatenate([normed[:, :tok], normed[:, tok:]], axis=0)
        send_buf[i] = (flat.T * gain).astype(jnp.bfloat16)

    for step in ((2, 6), (3, 7), (1, 5), (4, 0)):
        for j in step:
            finish(peers[j])
        for j in step:
            if j > 0:
                give_back(j).start()

    out_ref[:, pl.ds(pl.multiple_of(rank * 128, 128), 128)] = send_buf[rank]

    for j in range(1, GROUP):
        for kind in range(4):
            transfer(kind, j).wait_send()
        copy = give_back(j)
        copy.wait_send()
        copy.wait_recv()

    def drain_totals(j, _):
        for copy in exchange(j):
            copy.wait_send()
        return 0

    lax.fori_loop(1, groups, drain_totals, 0)


def on_device(queries, key_vectors, value_vectors, log_decay, routes, route_weight, out_gain):
    n_ctx, n_mem = lax.axis_size("ctx"), lax.axis_size("mem")
    tok, width = queries.shape
    heads = log_decay.shape[1]
    groups = n_ctx * n_mem // GROUP
    slots = n_mem + 1
    pad = (slots + 7) // 8 * 8
    gain = out_gain.reshape(GROUP, 1, 128)
    hbm = pl.BlockSpec(memory_space=pltpu.HBM)
    return pl.pallas_call(
        functools.partial(kernel, n_ctx, n_mem, heads, pad),
        out_shape=jax.ShapeDtypeStruct((tok, width), jnp.bfloat16),
        in_specs=[hbm] * 7,
        out_specs=pl.BlockSpec(memory_space=pltpu.VMEM),
        scratch_shapes=[
            pltpu.VMEM((GROUP, tok, 128), jnp.bfloat16),
            pltpu.VMEM((GROUP, tok, 128), jnp.bfloat16),
            pltpu.VMEM((GROUP, tok, 128), jnp.bfloat16),
            pltpu.VMEM((GROUP, 3 * pad, tok), jnp.float32),
            pltpu.VMEM((GROUP, 3 * pad, tok), jnp.float32),
            pltpu.VMEM((GROUP, 128, tok), jnp.bfloat16),
            pltpu.VMEM((GROUP, slots * 64, 128), jnp.float32),
            pltpu.VMEM((GROUP, pad, 128), jnp.float32),
            pltpu.VMEM((GROUP, pad, 128), jnp.float32),
            pltpu.VMEM((GROUP, 64, 2 * tok), jnp.float32),
            pltpu.VMEM((GROUP, tok, 128), jnp.bfloat16),
            pltpu.VMEM((groups, slots * 64, 128), jnp.bfloat16),
            pltpu.VMEM((groups, pad, 128), jnp.float32),
            pltpu.VMEM((heads, tok), jnp.bfloat16),
            pltpu.VMEM((2, tok), jnp.int32),
            pltpu.VMEM((2, tok), jnp.float32),
            pltpu.VMEM((GROUP, 1, 128), jnp.float32),
            pltpu.SemaphoreType.DMA((4, GROUP)),
            pltpu.SemaphoreType.DMA((4, GROUP)),
            pltpu.SemaphoreType.DMA((GROUP,)),
            pltpu.SemaphoreType.DMA((GROUP,)),
            pltpu.SemaphoreType.DMA((2, groups)),
            pltpu.SemaphoreType.DMA((2, groups)),
            pltpu.SemaphoreType.DMA((3,)),
            pltpu.SemaphoreType.DMA((4,)),
        ],
        compiler_params=pltpu.CompilerParams(
            collective_id=0, has_side_effects=True, vmem_limit_bytes=63 * 1024 * 1024
        ),
        cost_estimate=pl.CostEstimate(
            flops=2 * GROUP * 128 * 128 * 128 * 20, bytes_accessed=4 << 20, transcendentals=0
        ),
    )(queries, key_vectors, value_vectors, log_decay.T, routes.T, route_weight.T, gain)


def solution(mesh):
    rows = P(("ctx", "mem"), None)
    return jax.shard_map(
        on_device,
        mesh=mesh,
        in_specs=(rows, rows, rows, rows, rows, rows, P()),
        out_specs=rows,
        check_vma=False,
    )
```

time: 43.6 us -> 39 us (0.89)
  local copies, waits for them, and re-layouts: 5.54 us -> 1.67 us
    unnamed x15 -> x1, local copies, waits for them, and re-layouts: 5.46 us -> 1.67 us
where the time goes in v1:
time: 39 us; the launch traced here: 38.8 us
  Pallas kernels  37.2 us (95%)
  local copies, waits for them, and re-layouts  1.67 us (4%)
    pallas_call x1, Pallas kernels, on_device(): pl.pallas_call(functools.partial(kernel, n_ctx, n_mem, heads, pad), out_s...  37.2 us
    unnamed x1, local copies, waits for them, and re-layouts  1.67 us

profile of v1, /device:TPU:0, one launch (start us, length us, event | category | flops | bytes accessed | tf_op | source)
XLA Modules:
  0.0 38.8 jit_solution(2566524169314303927)
XLA Ops:
  0.0 37.2 %shard_map.73 = bf16[128,1024]{1,0:T(8,128)(2,1)} custom-call(bf16[128,1024]{1,0:T(8,128)(2,1)} %q_ref.1, bf16[128,1024]{1,0:T(8,128)(2,1)} %k_ref.1, bf16[128,1024]{1,0:T(8,128)(2,1)} %v_ref.1, bf16[16,128]{1,0:T(8,128)(2,1)} %bitcast.4, s32[2,128]{1,0:T(2,128)} %bitcast.6, f32[2,128]{1,0:T(2,128)} %bitcast.7, f32[8,1,128]{2,1,0:T(1,128)} %bitcast.5), custom_call_target="tpu_custom_call" | custom-call | flops 671088640 | bytes 4194304 | tf_op jit(solution)/shard_map/pallas_call | solution.py:327
  37.2 1.7 %copy.9 = bf16[128,1024]{1,0:T(8,128)(2,1)} copy(bf16[128,1024]{1,0:T(8,128)(2,1)} %shard_map.73) | data formatting | bytes 524288

commit v2 on v1

--- a/solution.py
+++ b/solution.py
@@ -131,9 +131,8 @@
             device_id_type=MESH,
         )
 
-    far_first = (2, 6, 3, 7, 1, 5, 4)
-    for kinds in ((0, 1, 2), (3,)):
-        for j in far_first:
+    for kinds, order in (((0, 1, 2), (4, 2, 1, 6, 5, 3, 7)), ((3,), (2, 6, 3, 7, 1, 5, 4))):
+        for j in order:
             for kind in kinds:
                 transfer(kind, j).start()
 
@@ -149,7 +148,7 @@
         weight = tab[i, 2 * pad : 3 * pad, :]
         return [(tab[i, h * pad : (h + 1) * pad, :], weight) for h in range(2)]
 
-    steps = ((0, 4), (1, 5), (2, 6), (3, 7))
+    steps = ((0, 4), (2, 1), (6, 5), (3, 7))
 
     def gather_state(i):
         vt = vbuf[i].astype(jnp.float32).T
@@ -230,7 +229,7 @@
                 vt_buf[i, h * half : (h + 1) * half, :], part
             )
 
-    for step in steps:
+    def arrive_and_inside(step):
         for j in step:
             if j == 0:
                 own[2].wait()
@@ -238,6 +237,9 @@
                 transfer(3, j).wait_recv()
         for j in step:
             inside(peers[j])
+
+    back = ((2, 6), (3, 7), (1, 5), (4, 0))
+    arrive_and_inside(back[0])
 
     def await_totals(j, _):
         for copy in exchange(j):
@@ -256,8 +258,9 @@
             parts.append(jnp.where(g < group, new, before))
         return jnp.concatenate(parts, axis=0)
 
-    carry_buf = jnp.zeros((slots * half, 128), jnp.float32)
-    carried = lax.fori_loop(0, groups, carry, carry_buf)
+    carried = lax.fori_loop(
+        0, groups, carry, jnp.zeros((slots * half, 128), jnp.float32), unroll=groups <= 8
+    )
     gain = gain_buf[rank]
 
     def give_back(j):
@@ -291,14 +294,19 @@
         flat = jnp.concatenate([normed[:, :tok], normed[:, tok:]], axis=0)
         send_buf[i] = (flat.T * gain).astype(jnp.bfloat16)
 
-    for step in ((2, 6), (3, 7), (1, 5), (4, 0)):
+    for number, step in enumerate(back):
+        if number > 0:
+            arrive_and_inside(step)
         for j in step:
             finish(peers[j])
         for j in step:
             if j > 0:
                 give_back(j).start()
 
-    out_ref[:, pl.ds(pl.multiple_of(rank * 128, 128), 128)] = send_buf[rank]
+    keep_own = pltpu.make_async_copy(
+        send_buf.at[rank], columns(out_ref, rank), own_sem.at[3]
+    )
+    keep_own.start()
 
     for j in range(1, GROUP):
         for kind in range(4):
@@ -313,6 +321,7 @@
         return 0
 
     lax.fori_loop(1, groups, drain_totals, 0)
+    keep_own.wait()
 
 
 def on_device(queries, key_vectors, value_vectors, log_decay, routes, route_weight, out_gain):
@@ -328,7 +337,7 @@
         functools.partial(kernel, n_ctx, n_mem, heads, pad),
         out_shape=jax.ShapeDtypeStruct((tok, width), jnp.bfloat16),
         in_specs=[hbm] * 7,
-        out_specs=pl.BlockSpec(memory_space=pltpu.VMEM),
+        out_specs=hbm,
         scratch_shapes=[
             pltpu.VMEM((GROUP, tok, 128), jnp.bfloat16),
             pltpu.VMEM((GROUP, tok, 128), jnp.bfloat16),
@@ -353,7 +362,7 @@
             pltpu.SemaphoreType.DMA((GROUP,)),
             pltpu.SemaphoreType.DMA((2, groups)),
             pltpu.SemaphoreType.DMA((2, groups)),
-            pltpu.SemaphoreType.DMA((3,)),
+            pltpu.SemaphoreType.DMA((4,)),
             pltpu.SemaphoreType.DMA((4,)),
         ],
         compiler_params=pltpu.CompilerParams(

time: 39 us -> 38.1 us (0.977)
  Pallas kernels: 37.2 us -> 36.2 us
    pallas_call x1, Pallas kernels: 37.2 us -> 36.2 us  [on_device(): pl.pallas_call(functools.partial(kernel, n_ctx, n_mem, heads, pad), out_s...]
where the time goes in v2:
time: 38.1 us; the launch traced here: 37.9 us
  Pallas kernels  36.2 us (95%)
  local copies, waits for them, and re-layouts  1.67 us (4%)
    pallas_call x1, Pallas kernels, on_device(): pl.pallas_call(functools.partial(kernel, n_ctx, n_mem, heads, pad), out_s...  36.2 us
    unnamed x1, local copies, waits for them, and re-layouts  1.67 us

profile of v2, /device:TPU:0, one launch (start us, length us, event | category | flops | bytes accessed | tf_op | source)
XLA Modules:
  0.0 37.9 jit_solution(7190034286829145333)
XLA Ops:
  0.0 36.2 %shard_map.73 = bf16[128,1024]{1,0:T(8,128)(2,1)} custom-call(bf16[128,1024]{1,0:T(8,128)(2,1)} %q_ref.1, bf16[128,1024]{1,0:T(8,128)(2,1)} %k_ref.1, bf16[128,1024]{1,0:T(8,128)(2,1)} %v_ref.1, bf16[16,128]{1,0:T(8,128)(2,1)} %bitcast.4, s32[2,128]{1,0:T(2,128)} %bitcast.6, f32[2,128]{1,0:T(2,128)} %bitcast.7, f32[8,1,128]{2,1,0:T(1,128)} %bitcast.5), custom_call_target="tpu_custom_call" | custom-call | flops 671088640 | bytes 4194304 | tf_op jit(solution)/shard_map/pallas_call | solution.py:336
  36.2 1.7 %copy.9 = bf16[128,1024]{1,0:T(8,128)(2,1)} copy(bf16[128,1024]{1,0:T(8,128)(2,1)} %shard_map.73) | data formatting | bytes 524288

commit v3 on v2

--- a/solution.py
+++ b/solution.py
@@ -25,9 +25,9 @@
 def kernel(
     n_ctx, n_mem, n_heads, pad,
     q_ref, k_ref, v_ref, decay_ref, routes_ref, weight_ref, gain_ref, out_ref,
-    qbuf, kbuf, vbuf, tab_mine, tab, vt_buf, t_buf, fade_buf, pre_buf, inner_buf, send_buf,
+    qbuf, kvbuf, q_mine, kv_mine, tab_mine, tab, vt_buf, t_buf, fade_buf, pre_buf, inner_buf, send_buf,
     total_buf, keep_buf, decay_buf, routes_buf, weight_buf, gain_buf,
-    send_sem, recv_sem, out_send, out_recv, tot_send, tot_recv, own_sem, small_sem,
+    send_sem, recv_sem, out_send, out_recv, tot_send, tot_recv, own_sem, small_sem, stage_sem,
 ):
     slots = n_mem + 1
     groups = n_ctx * n_mem // GROUP
@@ -70,12 +70,21 @@
     def columns(ref, r):
         return ref.at[:, pl.ds(pl.multiple_of(r * 128, 128), 128)]
 
-    own = [
-        pltpu.make_async_copy(columns(src, rank), dst.at[rank], own_sem.at[i])
-        for i, (src, dst) in enumerate(((k_ref, kbuf), (v_ref, vbuf), (q_ref, qbuf)))
-    ]
-    for copy in own:
-        copy.start()
+    send_order = (4, 2, 1, 6, 5, 3, 7)
+    back = ((2, 6), (3, 7), (1, 5), (4, 0))
+
+    def stage(kind, j):
+        src = columns((k_ref, v_ref, q_ref)[kind], peers[j])
+        if kind == 2:
+            dst = qbuf.at[rank] if j == 0 else q_mine.at[peers[j]]
+        else:
+            dst = kvbuf.at[rank, kind] if j == 0 else kv_mine.at[peers[j], kind]
+        return pltpu.make_async_copy(src, dst, stage_sem.at[kind, j])
+
+    for kinds in ((0, 1), (2,)):
+        for j in send_order + (0,):
+            for kind in kinds:
+                stage(kind, j).start()
 
     barrier = pltpu.get_barrier_semaphore()
     for j in range(1, GROUP):
@@ -116,12 +125,11 @@
 
     def transfer(kind, j):
         to = peers[j]
-        src, dst = {
-            0: lambda: (tab_mine.at[to], tab.at[rank]),
-            1: lambda: (columns(k_ref, to), kbuf.at[rank]),
-            2: lambda: (columns(v_ref, to), vbuf.at[rank]),
-            3: lambda: (columns(q_ref, to), qbuf.at[rank]),
-        }[kind]()
+        src, dst = (
+            (tab_mine.at[to], tab.at[rank]),
+            (kv_mine.at[to], kvbuf.at[rank]),
+            (q_mine.at[to], qbuf.at[rank]),
+        )[kind]
         return pltpu.make_async_remote_copy(
             src_ref=src,
             dst_ref=dst,
@@ -131,10 +139,16 @@
             device_id_type=MESH,
         )
 
-    for kinds, order in (((0, 1, 2), (4, 2, 1, 6, 5, 3, 7)), ((3,), (2, 6, 3, 7, 1, 5, 4))):
-        for j in order:
-            for kind in kinds:
-                transfer(kind, j).start()
+    for j in send_order:
+        transfer(0, j).start()
+        for kind in range(2):
+            stage(kind, j).wait()
+        transfer(1, j).start()
+    for step in back:
+        for j in step:
+            if j > 0:
+                stage(2, j).wait()
+                transfer(2, j).start()
 
     tab[rank] = tab_mine[rank]
 
@@ -151,7 +165,7 @@
     steps = ((0, 4), (2, 1), (6, 5), (3, 7))
 
     def gather_state(i):
-        vt = vbuf[i].astype(jnp.float32).T
+        vt = kvbuf[i, 1].astype(jnp.float32).T
         vt_buf[i] = vt.astype(jnp.bfloat16)
         parts, fades = [], []
         for h, (cumul, weight) in enumerate(factors(i)):
@@ -163,16 +177,16 @@
             )
             fades.append(jnp.broadcast_to(jnp.exp(last), (pad, 128)))
         scaled = jnp.concatenate(parts, axis=1).astype(jnp.bfloat16)
-        t_buf[i] = mm(scaled, split(kbuf[i], 0))
+        t_buf[i] = mm(scaled, split(kvbuf[i, 0], 0))
         fade_buf[i] = jnp.where(left, fades[0], fades[1])
 
     for step in steps:
         for j in step:
             if j == 0:
-                own[0].wait()
-                own[1].wait()
+                for kind in range(2):
+                    stage(kind, 0).wait()
             else:
-                for kind in range(3):
+                for kind in range(2):
                     transfer(kind, j).wait_recv()
         for j in step:
             gather_state(peers[j])
@@ -213,7 +227,7 @@
     lax.fori_loop(1, groups, launch_totals, 0)
 
     def inside(i):
-        scores = mm(kbuf[i], split(qbuf[i], 0), NT)
+        scores = mm(kvbuf[i, 0], split(qbuf[i], 0), NT)
         for h, (cumul, weight) in enumerate(factors(i)):
             middle = 0.5 * cumul[:, tok - 1 : tok]
             read_hi, read_lo = halves(weight * jnp.exp(cumul - middle))
@@ -232,13 +246,12 @@
     def arrive_and_inside(step):
         for j in step:
             if j == 0:
-                own[2].wait()
+                stage(2, 0).wait()
             else:
-                transfer(3, j).wait_recv()
+                transfer(2, j).wait_recv()
         for j in step:
             inside(peers[j])
 
-    back = ((2, 6), (3, 7), (1, 5), (4, 0))
     arrive_and_inside(back[0])
 
     def await_totals(j, _):
@@ -304,12 +317,12 @@
                 give_back(j).start()
 
     keep_own = pltpu.make_async_copy(
-        send_buf.at[rank], columns(out_ref, rank), own_sem.at[3]
+        send_buf.at[rank], columns(out_ref, rank), own_sem.at[0]
     )
     keep_own.start()
 
     for j in range(1, GROUP):
-        for kind in range(4):
+        for kind in range(3):
             transfer(kind, j).wait_send()
         copy = give_back(j)
         copy.wait_send()
@@ -340,8 +353,9 @@
         out_specs=hbm,
         scratch_shapes=[
             pltpu.VMEM((GROUP, tok, 128), jnp.bfloat16),
+            pltpu.VMEM((GROUP, 2, tok, 128), jnp.bfloat16),
             pltpu.VMEM((GROUP, tok, 128), jnp.bfloat16),
-            pltpu.VMEM((GROUP, tok, 128), jnp.bfloat16),
+            pltpu.VMEM((GROUP, 2, tok, 128), jnp.bfloat16),
             pltpu.VMEM((GROUP, 3 * pad, tok), jnp.float32),
             pltpu.VMEM((GROUP, 3 * pad, tok), jnp.float32),
             pltpu.VMEM((GROUP, 128, tok), jnp.bfloat16),
@@ -356,14 +370,15 @@
             pltpu.VMEM((2, tok), jnp.int32),
             pltpu.VMEM((2, tok), jnp.float32),
             pltpu.VMEM((GROUP, 1, 128), jnp.float32),
-            pltpu.SemaphoreType.DMA((4, GROUP)),
-            pltpu.SemaphoreType.DMA((4, GROUP)),
+            pltpu.SemaphoreType.DMA((3, GROUP)),
+            pltpu.SemaphoreType.DMA((3, GROUP)),
             pltpu.SemaphoreType.DMA((GROUP,)),
             pltpu.SemaphoreType.DMA((GROUP,)),
             pltpu.SemaphoreType.DMA((2, groups)),
             pltpu.SemaphoreType.DMA((2, groups)),
+            pltpu.SemaphoreType.DMA((1,)),
             pltpu.SemaphoreType.DMA((4,)),
-            pltpu.SemaphoreType.DMA((4,)),
+            pltpu.SemaphoreType.DMA((3, GROUP)),
         ],
         compiler_params=pltpu.CompilerParams(
             collective_id=0, has_side_effects=True, vmem_limit_bytes=63 * 1024 * 1024

time: 38.1 us -> 38.1 us (level)
  no operation moved by 1% of the time
where the time goes in v3:
time: 38.1 us; the launch traced here: 37.9 us
  Pallas kernels  36.2 us (95%)
  local copies, waits for them, and re-layouts  1.67 us (4%)
    pallas_call x1, Pallas kernels, on_device(): pl.pallas_call(functools.partial(kernel, n_ctx, n_mem, heads, pad), out_s...  36.2 us
    unnamed x1, local copies, waits for them, and re-layouts  1.67 us

profile of v3, /device:TPU:0, one launch (start us, length us, event | category | flops | bytes accessed | tf_op | source)
XLA Modules:
  0.0 37.9 jit_solution(6938281792557531130)
XLA Ops:
  0.0 36.2 %shard_map.73 = bf16[128,1024]{1,0:T(8,128)(2,1)} custom-call(bf16[128,1024]{1,0:T(8,128)(2,1)} %q_ref.1, bf16[128,1024]{1,0:T(8,128)(2,1)} %k_ref.1, bf16[128,1024]{1,0:T(8,128)(2,1)} %v_ref.1, bf16[16,128]{1,0:T(8,128)(2,1)} %bitcast.4, s32[2,128]{1,0:T(2,128)} %bitcast.6, f32[2,128]{1,0:T(2,128)} %bitcast.7, f32[8,1,128]{2,1,0:T(1,128)} %bitcast.5), custom_call_target="tpu_custom_call" | custom-call | flops 671088640 | bytes 4194304 | tf_op jit(solution)/shard_map/pallas_call | solution.py:349
  36.2 1.7 %copy.9 = bf16[128,1024]{1,0:T(8,128)(2,1)} copy(bf16[128,1024]{1,0:T(8,128)(2,1)} %shard_map.73) | data formatting | bytes 524288

commit v4 on v3

--- a/solution.py
+++ b/solution.py
@@ -25,7 +25,7 @@
 def kernel(
     n_ctx, n_mem, n_heads, pad,
     q_ref, k_ref, v_ref, decay_ref, routes_ref, weight_ref, gain_ref, out_ref,
-    qbuf, kvbuf, q_mine, kv_mine, tab_mine, tab, vt_buf, t_buf, fade_buf, pre_buf, inner_buf, send_buf,
+    qbuf, kvbuf, q_mine, kv_mine, tab_mine, tab, cum_buf, vt_buf, t_buf, fade_buf, pre_buf, inner_buf, send_buf,
     total_buf, keep_buf, decay_buf, routes_buf, weight_buf, gain_buf,
     send_sem, recv_sem, out_send, out_recv, tot_send, tot_recv, own_sem, small_sem, stage_sem,
 ):
@@ -102,24 +102,20 @@
     col = lax.broadcasted_iota(jnp.int32, (tok, tok), 1)
     causal = row <= col
     upper = jnp.where(causal, 1.0, 0.0).astype(jnp.bfloat16)
-    tab_mine[...] = jnp.zeros_like(tab_mine)
     for copy in small:
         copy.wait()
     decay = decay_buf[...].astype(jnp.float32)
     first, second = routes_buf[0:1, :], routes_buf[1:2, :]
     w_first, w_second = weight_buf[0:1, :], weight_buf[1:2, :]
-    for m in range(slots):
-        if m == 0:
-            masked, weight = decay, jnp.ones_like(w_first)
-        else:
-            in_first, in_second = first == m - 1, second == m - 1
-            masked = jnp.where(in_first | in_second, decay, 0.0)
-            weight = jnp.where(in_first, w_first, jnp.where(in_second, w_second, 0.0))
-        cumul = mm(masked.astype(jnp.bfloat16), upper)
-        for p in range(GROUP):
-            for h in range(2):
-                tab_mine[p, h * pad + m : h * pad + m + 1, :] = cumul[2 * p + h : 2 * p + h + 1, :]
-            tab_mine[p, 2 * pad + m : 2 * pad + m + 1, :] = weight
+    weights = [jnp.ones_like(w_first)] + [
+        jnp.where(first == m, w_first, jnp.where(second == m, w_second, 0.0))
+        for m in range(n_mem)
+    ]
+    tab_mine[...] = jnp.zeros_like(tab_mine)
+    for p in range(GROUP):
+        for m in range(slots):
+            tab_mine[p, m : m + 1, :] = weights[m]
+        tab_mine[p, slots : slots + 2, :] = decay[2 * p : 2 * p + 2, :]
 
     pl.semaphore_wait(barrier, GROUP - 1 + groups - 1)
 
@@ -159,12 +155,17 @@
         return jnp.concatenate([jnp.where(left, x, zero), jnp.where(left, zero, x)], axis=axis)
 
     def factors(i):
-        weight = tab[i, 2 * pad : 3 * pad, :]
-        return [(tab[i, h * pad : (h + 1) * pad, :], weight) for h in range(2)]
+        weight = tab[i]
+        return [(cum_buf[i, h * pad : (h + 1) * pad, :], weight) for h in range(2)]
 
     steps = ((0, 4), (2, 1), (6, 5), (3, 7))
 
     def gather_state(i):
+        member = tab[i] > 0.0
+        masked = [
+            jnp.where(member, tab[i, slots + h : slots + h + 1, :], 0.0) for h in range(2)
+        ]
+        cum_buf[i] = mm(jnp.concatenate(masked, axis=0).astype(jnp.bfloat16), upper)
         vt = kvbuf[i, 1].astype(jnp.float32).T
         vt_buf[i] = vt.astype(jnp.bfloat16)
         parts, fades = [], []
@@ -191,40 +192,43 @@
         for j in step:
             gather_state(peers[j])
 
+    def exchange(j, part):
+        if part == slots:
+            mine = keep_buf.at[group]
+        else:
+            mine = total_buf.at[group, pl.ds(part * half, half)]
+        return pltpu.make_async_remote_copy(
+            src_ref=mine,
+            dst_ref=mine,
+            send_sem=tot_send.at[part, j],
+            recv_sem=tot_recv.at[part, j],
+            device_id=device(other(j) * GROUP + rank),
+            device_id_type=MESH,
+        )
+
+    def each_group(part, act):
+        def run(j, _):
+            act(exchange(j, part))
+            return 0
+
+        lax.fori_loop(1, groups, run, 0)
+
+    kept = jnp.ones((pad, 128), jnp.float32)
+    for i in range(GROUP):
+        pre_buf[i] = kept
+        kept = kept * fade_buf[i]
+    keep_buf[group] = kept
+    each_group(slots, lambda copy: copy.start())
     for m in range(slots):
         rows = pl.ds(m * half, half)
-        state = jnp.zeros((half, 128), jnp.float32)
-        kept = jnp.ones((1, 128), jnp.float32)
-        for i in range(GROUP):
-            fade = fade_buf[i, m : m + 1, :]
+        state = t_buf[0, rows, :]
+        t_buf[0, rows, :] = jnp.zeros((half, 128), jnp.float32)
+        for i in range(1, GROUP):
             added = t_buf[i, rows, :]
             t_buf[i, rows, :] = state
-            pre_buf[i, m : m + 1, :] = kept
-            state = fade * state + added
-            kept = kept * fade
+            state = fade_buf[i, m : m + 1, :] * state + added
         total_buf[group, rows, :] = state.astype(jnp.bfloat16)
-        keep_buf[group, m : m + 1, :] = kept
-
-    def exchange(j):
-        to = device(other(j) * GROUP + rank)
-        return [
-            pltpu.make_async_remote_copy(
-                src_ref=ref.at[group],
-                dst_ref=ref.at[group],
-                send_sem=tot_send.at[kind, j],
-                recv_sem=tot_recv.at[kind, j],
-                device_id=to,
-                device_id_type=MESH,
-            )
-            for kind, ref in enumerate((total_buf, keep_buf))
-        ]
-
-    def launch_totals(j, _):
-        for copy in exchange(j):
-            copy.start()
-        return 0
-
-    lax.fori_loop(1, groups, launch_totals, 0)
+        each_group(m, lambda copy: copy.start())
 
     def inside(i):
         scores = mm(kvbuf[i, 0], split(qbuf[i], 0), NT)
@@ -254,26 +258,21 @@
 
     arrive_and_inside(back[0])
 
-    def await_totals(j, _):
-        for copy in exchange(j):
-            copy.wait_recv()
-        return 0
-
-    lax.fori_loop(1, groups, await_totals, 0)
-
-    def carry(g, state):
-        parts = []
-        for m in range(slots):
-            before = state[m * half : (m + 1) * half, :]
-            new = keep_buf[g, m : m + 1, :] * before + total_buf[
-                g, m * half : (m + 1) * half, :
-            ].astype(jnp.float32)
-            parts.append(jnp.where(g < group, new, before))
-        return jnp.concatenate(parts, axis=0)
-
-    carried = lax.fori_loop(
-        0, groups, carry, jnp.zeros((slots * half, 128), jnp.float32), unroll=groups <= 8
-    )
+    each_group(slots, lambda copy: copy.wait_recv())
+    carried = []
+    for m in range(slots):
+        each_group(m, lambda copy: copy.wait_recv())
+
+        def carry(g, before, m=m):
+            added = total_buf[g, m * half : (m + 1) * half, :].astype(jnp.float32)
+            new = keep_buf[g, m : m + 1, :] * before + added
+            return jnp.where(g < group, new, before)
+
+        carried.append(
+            lax.fori_loop(
+                0, groups, carry, jnp.zeros((half, 128), jnp.float32), unroll=groups <= 8
+            )
+        )
     gain = gain_buf[rank]
 
     def give_back(j):
@@ -290,7 +289,7 @@
         state = jnp.concatenate(
             [
                 t_buf[i, m * half : (m + 1) * half, :]
-                + pre_buf[i, m : m + 1, :] * carried[m * half : (m + 1) * half, :]
+                + pre_buf[i, m : m + 1, :] * carried[m]
                 for m in range(slots)
             ],
             axis=0,
@@ -328,12 +327,8 @@
         copy.wait_send()
         copy.wait_recv()
 
-    def drain_totals(j, _):
-        for copy in exchange(j):
-            copy.wait_send()
-        return 0
-
-    lax.fori_loop(1, groups, drain_totals, 0)
+    for part in range(slots + 1):
+        each_group(part, lambda copy: copy.wait_send())
     keep_own.wait()
 
 
@@ -343,7 +338,7 @@
     heads = log_decay.shape[1]
     groups = n_ctx * n_mem // GROUP
     slots = n_mem + 1
-    pad = (slots + 7) // 8 * 8
+    pad = (slots + 9) // 8 * 8
     gain = out_gain.reshape(GROUP, 1, 128)
     hbm = pl.BlockSpec(memory_space=pltpu.HBM)
     return pl.pallas_call(
@@ -356,8 +351,9 @@
             pltpu.VMEM((GROUP, 2, tok, 128), jnp.bfloat16),
             pltpu.VMEM((GROUP, tok, 128), jnp.bfloat16),
             pltpu.VMEM((GROUP, 2, tok, 128), jnp.bfloat16),
-            pltpu.VMEM((GROUP, 3 * pad, tok), jnp.float32),
-            pltpu.VMEM((GROUP, 3 * pad, tok), jnp.float32),
+            pltpu.VMEM((GROUP, pad, tok), jnp.float32),
+            pltpu.VMEM((GROUP, pad, tok), jnp.float32),
+            pltpu.VMEM((GROUP, 2 * pad, tok), jnp.float32),
             pltpu.VMEM((GROUP, 128, tok), jnp.bfloat16),
             pltpu.VMEM((GROUP, slots * 64, 128), jnp.float32),
             pltpu.VMEM((GROUP, pad, 128), jnp.float32),
@@ -374,8 +370,8 @@
             pltpu.SemaphoreType.DMA((3, GROUP)),
             pltpu.SemaphoreType.DMA((GROUP,)),
             pltpu.SemaphoreType.DMA((GROUP,)),
-            pltpu.SemaphoreType.DMA((2, groups)),
-            pltpu.SemaphoreType.DMA((2, groups)),
+            pltpu.SemaphoreType.DMA((slots + 1, groups)),
+            pltpu.SemaphoreType.DMA((slots + 1, groups)),
             pltpu.SemaphoreType.DMA((1,)),
             pltpu.SemaphoreType.DMA((4,)),
             pltpu.SemaphoreType.DMA((3, GROUP)),

time: 38.1 us -> 37.4 us (0.982)
  Pallas kernels: 36.2 us -> 35.4 us
    pallas_call x1, Pallas kernels: 36.2 us -> 35.4 us  [on_device(): pl.pallas_call(functools.partial(kernel, n_ctx, n_mem, heads, pad), out_s...]
where the time goes in v4:
time: 37.4 us; the launch traced here: 37.1 us
  Pallas kernels  35.4 us (95%)
  local copies, waits for them, and re-layouts  1.67 us (4%)
    pallas_call x1, Pallas kernels, on_device(): pl.pallas_call(functools.partial(kernel, n_ctx, n_mem, heads, pad), out_s...  35.4 us
    unnamed x1, local copies, waits for them, and re-layouts  1.67 us

profile of v4, /device:TPU:0, one launch (start us, length us, event | category | flops | bytes accessed | tf_op | source)
XLA Modules:
  0.0 37.1 jit_solution(9650014571119706768)
XLA Ops:
  0.0 35.4 %shard_map.73 = bf16[128,1024]{1,0:T(8,128)(2,1)} custom-call(bf16[128,1024]{1,0:T(8,128)(2,1)} %q_ref.1, bf16[128,1024]{1,0:T(8,128)(2,1)} %k_ref.1, bf16[128,1024]{1,0:T(8,128)(2,1)} %v_ref.1, bf16[16,128]{1,0:T(8,128)(2,1)} %bitcast.4, s32[2,128]{1,0:T(2,128)} %bitcast.6, f32[2,128]{1,0:T(2,128)} %bitcast.7, f32[8,1,128]{2,1,0:T(1,128)} %bitcast.5), custom_call_target="tpu_custom_call" | custom-call | flops 671088640 | bytes 4194304 | tf_op jit(solution)/shard_map/pallas_call | solution.py:344
  35.5 1.7 %copy.9 = bf16[128,1024]{1,0:T(8,128)(2,1)} copy(bf16[128,1024]{1,0:T(8,128)(2,1)} %shard_map.73) | data formatting | bytes 524288

commit v5 on v4

--- a/solution.py
+++ b/solution.py
@@ -53,6 +53,18 @@
     def other(j):
         return lax.rem(group + j, groups)
 
+    barrier = pltpu.get_barrier_semaphore()
+    for j in range(1, GROUP):
+        pl.semaphore_signal(barrier, inc=1, device_id=devices[j], device_id_type=MESH)
+
+    def greet_group(j, _):
+        pl.semaphore_signal(
+            barrier, inc=1, device_id=device(other(j) * GROUP + rank), device_id_type=MESH
+        )
+        return 0
+
+    lax.fori_loop(1, groups, greet_group, 0)
+
     small = [
         pltpu.make_async_copy(src, dst, small_sem.at[i])
         for i, (src, dst) in enumerate(
@@ -81,22 +93,9 @@
             dst = kvbuf.at[rank, kind] if j == 0 else kv_mine.at[peers[j], kind]
         return pltpu.make_async_copy(src, dst, stage_sem.at[kind, j])
 
-    for kinds in ((0, 1), (2,)):
-        for j in send_order + (0,):
-            for kind in kinds:
-                stage(kind, j).start()
-
-    barrier = pltpu.get_barrier_semaphore()
-    for j in range(1, GROUP):
-        pl.semaphore_signal(barrier, inc=1, device_id=devices[j], device_id_type=MESH)
-
-    def greet_group(j, _):
-        pl.semaphore_signal(
-            barrier, inc=1, device_id=device(other(j) * GROUP + rank), device_id_type=MESH
-        )
-        return 0
-
-    lax.fori_loop(1, groups, greet_group, 0)
+    for j in send_order + (0,):
+        for kind in range(2):
+            stage(kind, j).start()
 
     row = lax.broadcasted_iota(jnp.int32, (tok, tok), 0)
     col = lax.broadcasted_iota(jnp.int32, (tok, tok), 1)
@@ -142,6 +141,9 @@
         transfer(1, j).start()
     for step in back:
         for j in step:
+            stage(2, j).start()
+    for step in back:
+        for j in step:
             if j > 0:
                 stage(2, j).wait()
                 transfer(2, j).start()
@@ -256,7 +258,8 @@
         for j in step:
             inside(peers[j])
 
-    arrive_and_inside(back[0])
+    for step in back:
+        arrive_and_inside(step)
 
     each_group(slots, lambda copy: copy.wait_recv())
     carried = []
@@ -306,9 +309,7 @@
         flat = jnp.concatenate([normed[:, :tok], normed[:, tok:]], axis=0)
         send_buf[i] = (flat.T * gain).astype(jnp.bfloat16)
 
-    for number, step in enumerate(back):
-        if number > 0:
-            arrive_and_inside(step)
+    for step in back:
         for j in step:
             finish(peers[j])
         for j in step:

time: 37.4 us -> 38.3 us (1.024)
  Pallas kernels: 35.4 us -> 36.4 us
    pallas_call x1, Pallas kernels: 35.4 us -> 36.4 us  [on_device(): pl.pallas_call(functools.partial(kernel, n_ctx, n_mem, heads, pad), out_s...]
where the time goes in v5:
time: 38.3 us; the launch traced here: 38 us
  Pallas kernels  36.4 us (95%)
  local copies, waits for them, and re-layouts  1.67 us (4%)
    pallas_call x1, Pallas kernels, on_device(): pl.pallas_call(functools.partial(kernel, n_ctx, n_mem, heads, pad), out_s...  36.4 us
    unnamed x1, local copies, waits for them, and re-layouts  1.67 us

profile of v5, /device:TPU:0, one launch (start us, length us, event | category | flops | bytes accessed | tf_op | source)
XLA Modules:
  0.0 38.0 jit_solution(2371369665127661176)
XLA Ops:
  0.0 36.4 %shard_map.73 = bf16[128,1024]{1,0:T(8,128)(2,1)} custom-call(bf16[128,1024]{1,0:T(8,128)(2,1)} %q_ref.1, bf16[128,1024]{1,0:T(8,128)(2,1)} %k_ref.1, bf16[128,1024]{1,0:T(8,128)(2,1)} %v_ref.1, bf16[16,128]{1,0:T(8,128)(2,1)} %bitcast.4, s32[2,128]{1,0:T(2,128)} %bitcast.6, f32[2,128]{1,0:T(2,128)} %bitcast.7, f32[8,1,128]{2,1,0:T(1,128)} %bitcast.5), custom_call_target="tpu_custom_call" | custom-call | flops 671088640 | bytes 4194304 | tf_op jit(solution)/shard_map/pallas_call | solution.py:345
  36.4 1.7 %copy.9 = bf16[128,1024]{1,0:T(8,128)(2,1)} copy(bf16[128,1024]{1,0:T(8,128)(2,1)} %shard_map.73) | data formatting | bytes 524288

commit v6 on v5

--- a/solution.py
+++ b/solution.py
@@ -258,8 +258,7 @@
         for j in step:
             inside(peers[j])
 
-    for step in back:
-        arrive_and_inside(step)
+    arrive_and_inside(back[0])
 
     each_group(slots, lambda copy: copy.wait_recv())
     carried = []
@@ -309,7 +308,9 @@
         flat = jnp.concatenate([normed[:, :tok], normed[:, tok:]], axis=0)
         send_buf[i] = (flat.T * gain).astype(jnp.bfloat16)
 
-    for step in back:
+    for number, step in enumerate(back):
+        if number > 0:
+            arrive_and_inside(step)
         for j in step:
             finish(peers[j])
         for j in step:

time: 38.3 us -> 37.4 us (0.977)
  Pallas kernels: 36.4 us -> 35.4 us
    pallas_call x1, Pallas kernels: 36.4 us -> 35.4 us  [on_device(): pl.pallas_call(functools.partial(kernel, n_ctx, n_mem, heads, pad), out_s...]
where the time goes in v6:
time: 37.4 us; the launch traced here: 37.1 us
  Pallas kernels  35.4 us (95%)
  local copies, waits for them, and re-layouts  1.67 us (4%)
    pallas_call x1, Pallas kernels, on_device(): pl.pallas_call(functools.partial(kernel, n_ctx, n_mem, heads, pad), out_s...  35.4 us
    unnamed x1, local copies, waits for them, and re-layouts  1.67 us

profile of v6, /device:TPU:0, one launch (start us, length us, event | category | flops | bytes accessed | tf_op | source)
XLA Modules:
  0.0 37.1 jit_solution(12626147029735079064)
XLA Ops:
  0.0 35.4 %shard_map.73 = bf16[128,1024]{1,0:T(8,128)(2,1)} custom-call(bf16[128,1024]{1,0:T(8,128)(2,1)} %q_ref.1, bf16[128,1024]{1,0:T(8,128)(2,1)} %k_ref.1, bf16[128,1024]{1,0:T(8,128)(2,1)} %v_ref.1, bf16[16,128]{1,0:T(8,128)(2,1)} %bitcast.4, s32[2,128]{1,0:T(2,128)} %bitcast.6, f32[2,128]{1,0:T(2,128)} %bitcast.7, f32[8,1,128]{2,1,0:T(1,128)} %bitcast.5), custom_call_target="tpu_custom_call" | custom-call | flops 671088640 | bytes 4194304 | tf_op jit(solution)/shard_map/pallas_call | solution.py:346
  35.4 1.7 %copy.9 = bf16[128,1024]{1,0:T(8,128)(2,1)} copy(bf16[128,1024]{1,0:T(8,128)(2,1)} %shard_map.73) | data formatting | bytes 524288

commit v7 on v6

--- a/solution.py
+++ b/solution.py
@@ -9,6 +9,7 @@
 
 MESH = pl.DeviceIdType.MESH
 GROUP = 8
+PIECES = 8
 NT = (((1,), (1,)), ((), ()))
 TN = (((0,), (0,)), ((), ()))
 
@@ -83,7 +84,7 @@
         return ref.at[:, pl.ds(pl.multiple_of(r * 128, 128), 128)]
 
     send_order = (4, 2, 1, 6, 5, 3, 7)
-    back = ((2, 6), (3, 7), (1, 5), (4, 0))
+    back = ((4, 0), (2, 6), (3, 7), (1, 5))
 
     def stage(kind, j):
         src = columns((k_ref, v_ref, q_ref)[kind], peers[j])
@@ -334,6 +335,20 @@
     keep_own.wait()
 
 
+def hand_over(src_ref, dst_ref, sem):
+    rows = src_ref.shape[0] // PIECES
+    copies = [
+        pltpu.make_async_copy(
+            src_ref.at[pl.ds(i * rows, rows)], dst_ref.at[pl.ds(i * rows, rows)], sem.at[i]
+        )
+        for i in range(PIECES)
+    ]
+    for copy in copies:
+        copy.start()
+    for copy in copies:
+        copy.wait()
+
+
 def on_device(queries, key_vectors, value_vectors, log_decay, routes, route_weight, out_gain):
     n_ctx, n_mem = lax.axis_size("ctx"), lax.axis_size("mem")
     tok, width = queries.shape
@@ -343,7 +358,7 @@
     pad = (slots + 9) // 8 * 8
     gain = out_gain.reshape(GROUP, 1, 128)
     hbm = pl.BlockSpec(memory_space=pltpu.HBM)
-    return pl.pallas_call(
+    mixed = pl.pallas_call(
         functools.partial(kernel, n_ctx, n_mem, heads, pad),
         out_shape=jax.ShapeDtypeStruct((tok, width), jnp.bfloat16),
         in_specs=[hbm] * 7,
@@ -385,6 +400,14 @@
             flops=2 * GROUP * 128 * 128 * 128 * 20, bytes_accessed=4 << 20, transcendentals=0
         ),
     )(queries, key_vectors, value_vectors, log_decay.T, routes.T, route_weight.T, gain)
+    return pl.pallas_call(
+        hand_over,
+        out_shape=jax.ShapeDtypeStruct((tok, width), jnp.bfloat16),
+        in_specs=[hbm],
+        out_specs=hbm,
+        scratch_shapes=[pltpu.SemaphoreType.DMA((PIECES,))],
+        compiler_params=pltpu.CompilerParams(vmem_limit_bytes=63 * 1024 * 1024),
+    )(mixed)
 
 
 def solution(mesh):

time: 37.4 us -> 45.9 us (1.23)
  Pallas kernels: 35.4 us -> 45.6 us
  local copies, waits for them, and re-layouts: 1.67 us -> 0 us
    pallas_call x0 -> x1, Pallas kernels: none -> 9.12 us  [on_device(): pl.pallas_call(hand_over, out_shape=jax.ShapeDtypeStruct((tok, width), jn...]
    unnamed x1 -> x0, local copies, waits for them, and re-layouts: 1.67 us -> none
    pallas_call x1, Pallas kernels: 35.4 us -> 36.5 us  [on_device(): pl.pallas_call(functools.partial(kernel, n_ctx, n_mem, heads, pad), out_s...]
where the time goes in v7:
time: 45.9 us; the launch traced here: 45.6 us
  Pallas kernels  45.6 us (99%)
    pallas_call x1, Pallas kernels, on_device(): pl.pallas_call(functools.partial(kernel, n_ctx, n_mem, heads, pad), out_s...  36.5 us
    pallas_call x1, Pallas kernels, on_device(): pl.pallas_call(hand_over, out_shape=jax.ShapeDtypeStruct((tok, width), jn...  9.12 us

profile of v7, /device:TPU:0, one launch (start us, length us, event | category | flops | bytes accessed | tf_op | source)
XLA Modules:
  0.0 45.6 jit_solution(9515658826874577563)
XLA Ops:
  0.0 36.5 %shard_map.73.src_ref = bf16[128,1024]{1,0:T(8,128)(2,1)} custom-call(bf16[128,1024]{1,0:T(8,128)(2,1)} %q_ref.1, bf16[128,1024]{1,0:T(8,128)(2,1)} %k_ref.1, bf16[128,1024]{1,0:T(8,128)(2,1)} %v_ref.1, bf16[16,128]{1,0:T(8,128)(2,1)} %bitcast.4, s32[2,128]{1,0:T(2,128)} %bitcast.6, f32[2,128]{1,0:T(2,128)} %bitcast.7, f32[8,1,128]{2,1,0:T(1,128)} %bitcast.5), custom_call_target="tpu_custom_call" | custom-call | flops 671088640 | bytes 4194304 | tf_op jit(solution)/shard_map/pallas_call | solution.py:361
  36.5 9.1 %shard_map.74 = bf16[128,1024]{1,0:T(8,128)(2,1)} custom-call(bf16[128,1024]{1,0:T(8,128)(2,1)} %shard_map.73.src_ref), custom_call_target="tpu_custom_call" | custom-call | tf_op jit(solution)/shard_map/pallas_call | solution.py:403
